TPU v7x, 1024 devices: a whole 4x4x32 slice. The times are simulated.
1024 devices in a mesh: dp: 32 (over z), dom: 2 (over x_hi), mp: 16 (over x_lo, y, core).
Axes of the slice: x: 4 (x_hi: 2, x_lo: 2; x = x_hi * 2 + x_lo), y: 4, z: 32, core: 2. Of those that a mesh axis runs over, the one named last changes fastest.
Arguments:
- img_embed: bfloat16 [16384, 1152], P('dp'), may hold values from -43 to 43
- txt_embed: bfloat16 [16384, 1152], P(('dom', 'mp')), may hold values from -43 to 43
- img_feats: bfloat16 [16384, 1152], P('dp'), may hold values from -6 to 6
- txt_feats: bfloat16 [16384, 1152], P(('dom', 'mp')), may hold values from -6 to 6
- img_ids: int32 [16384], P('dp'), may hold values from 0 to 2047, as said below
- txt_ids: int32 [16384], P(('dom', 'mp')), may hold values from 0 to 2047
- loss_params: float32 [3], replicated, as said below
Outputs:
- img_weight_grad: float32 [1152, 1152], P('dp', ('dom', 'mp'))
- txt_weight_grad: float32 [1152, 1152], P(('dom', 'mp'), 'dp')
Inputs may be any that keep to these rules, and one draw needn't show every extreme that they name: `img_ids`: an image row and a text row form a positive pair exactly when their labels are equal. `loss_params`: entry 0 is the logit scale in 8 to 14, entry 1 the logit bias in -6 to -2, entry 2 the cotangent, positive.
All inputs are finite; a program needn't handle non-finite values.
Results may differ from a plain program's by a relative error of at most 0.0035.
Values may be sent and summed in bfloat16 or wider, within the bound.
No kernel may reach another device: no remote copies, remote signals or barrier semaphores. Data moves between devices by JAX's collectives and lax.ppermute only.
A program may use at most 32 MiB of HBM per device.

v0:
```python
import jax
import jax.numpy as jnp
from jax import lax
from jax.sharding import PartitionSpec as P


def unit_rows(embedded):
    values = embedded.astype(jnp.float32)
    length = jnp.sqrt(jnp.sum(values * values, axis=1, keepdims=True) + 1e-06)
    return ((values / length).astype(jnp.bfloat16), length)


def per_device(img_embed, txt_embed, img_feats, txt_feats, img_ids, txt_ids, loss_params):
    img_unit, img_length = unit_rows(img_embed)
    txt_unit, txt_length = unit_rows(txt_embed)
    scale_t = loss_params[0]
    shift_b = loss_params[1]
    cotangent = loss_params[2]
    group_size = lax.axis_size(("dom", "mp"))
    loop_size = lax.axis_size("dp")
    pairs_total = img_embed.shape[0] * loop_size
    similar = lax.dot_general(
        img_unit, txt_unit, (((1,), (1,)), ((), ())), preferred_element_type=jnp.float32
    )
    pair_sign = jnp.where(img_ids[:, None] == txt_ids[None, :], 1.0, -1.0).astype(jnp.float32)
    logits = scale_t * similar + shift_b
    weights = (
        scale_t * (-cotangent / pairs_total) * pair_sign * jax.nn.sigmoid(-pair_sign * logits)
    ).astype(jnp.bfloat16)
    image_count = img_unit.shape[0] // group_size
    sliced = weights
    image_grad = lax.psum_scatter(
        jnp.dot(sliced, txt_unit, preferred_element_type=jnp.float32),
        ("dom", "mp"),
        scatter_dimension=0,
        tiled=True,
    )
    image_offset = lax.axis_index(("dom", "mp")) * image_count
    image_values = lax.dynamic_slice_in_dim(img_unit, image_offset, image_count, 0).astype(
        jnp.float32
    )
    image_length = lax.dynamic_slice_in_dim(img_length, image_offset, image_count, 0)
    image_radial = jnp.sum(image_values * image_grad, axis=1, keepdims=True)
    image_dz = ((image_grad - image_values * image_radial) / image_length).astype(jnp.bfloat16)
    image_cols = lax.all_to_all(image_dz, ("dom", "mp"), split_axis=1, concat_axis=0, tiled=True)
    text_count = txt_unit.shape[0] // loop_size
    sliced = weights
    text_grad = lax.psum_scatter(
        lax.dot_general(
            sliced, img_unit, (((0,), (0,)), ((), ())), preferred_element_type=jnp.float32
        ),
        "dp",
        scatter_dimension=0,
        tiled=True,
    )
    text_offset = lax.axis_index("dp") * text_count
    text_values = lax.dynamic_slice_in_dim(txt_unit, text_offset, text_count, 0).astype(jnp.float32)
    text_length = lax.dynamic_slice_in_dim(txt_length, text_offset, text_count, 0)
    text_radial = jnp.sum(text_values * text_grad, axis=1, keepdims=True)
    text_dz = ((text_grad - text_values * text_radial) / text_length).astype(jnp.bfloat16)
    text_cols = lax.all_to_all(text_dz, "dp", split_axis=1, concat_axis=0, tiled=True)
    sliced = img_feats
    img_weight_grad = lax.psum_scatter(
        lax.dot_general(
            sliced, image_cols, (((0,), (0,)), ((), ())), preferred_element_type=jnp.float32
        ),
        "dp",
        scatter_dimension=0,
        tiled=True,
    )
    sliced = txt_feats
    txt_weight_grad = lax.psum_scatter(
        lax.dot_general(
            sliced, text_cols, (((0,), (0,)), ((), ())), preferred_element_type=jnp.float32
        ),
        ("dom", "mp"),
        scatter_dimension=0,
        tiled=True,
    )
    return (img_weight_grad, txt_weight_grad)


def solution(mesh):
    return jax.shard_map(
        per_device,
        mesh=mesh,
        in_specs=(
            P("dp", None),
            P(("dom", "mp"), None),
            P("dp", None),
            P(("dom", "mp"), None),
            P("dp"),
            P(("dom", "mp")),
            P(),
        ),
        out_specs=(P("dp", ("dom", "mp")), P(("dom", "mp"), "dp")),
        check_vma=False,
    )
```

profile of v0, /device:TPU:6, one launch (start us, length us, event | category | flops | bytes accessed | tf_op | source)
XLA Modules:
  0.0 761.2 jit_solution(11633614938294333603)
XLA Ops:
  7.2 0.0 copy-start
  7.2 0.0 copy-start.1
  7.2 0.0 reduce-scatter.5.cloned.1.call-start
  7.2 1.4 fusion.20
  9.3 1.6 fusion
  10.9 0.3 fusion.2
  11.9 0.0 copy-start.4
  11.9 2.5 fusion.1
  14.4 2.4 fusion.11
  16.8 0.8 copy-done.2
  17.6 2.3 fusion.21
  19.8 0.0 reduce-scatter.5.cloned.1.call-update
  19.9 0.0 reduce-scatter.7.cloned.1.call-start
  19.9 3.3 fusion.22
  23.2 0.0 reduce-scatter.7.cloned.1.call-update
  23.3 0.1 dynamic-slice.6
  23.3 0.1 dynamic-slice.7
  23.4 137.1 %reduce-scatter.5.cloned.1.call-done = f32[16,1152]{1,0:T(8,128)} async-done(((f32[512,1152]{1,0:T(8,128)}), f32[16,1152]{1,0:T(8,128)}) %reduce-scatter.5.cloned.1.call-update) | async-done | bytes 73744 | tf_op jit(solution)/shard_map/reduce_scatter | solution.py:32
  160.6 1.0 fusion.12
  161.6 1.6 fusion.15
  163.1 1.1 all_to_all.28
  164.3 0.1 copy.26
  164.3 0.8 reshape.57
  165.1 5.7 all-to-all-start
  170.8 131.0 %reduce-scatter.7.cloned.1.call-done = f32[16,1152]{1,0:T(8,128)} async-done(((f32[512,1152]{1,0:T(8,128)}), f32[16,1152]{1,0:T(8,128)}) %reduce-scatter.7.cloned.1.call-update) | async-done | bytes 73744 | tf_op jit(solution)/shard_map/reduce_scatter | solution.py:48
  301.8 1.0 fusion.16
  302.8 1.0 fusion.19
  303.8 0.3 all_to_all.32
  304.1 0.1 copy.25
  304.2 0.8 reshape.59
  305.0 17.1 %all-to-all-start.1 = ((bf16[32,2,288]{2,1,0:T(2,128)(2,1)}), bf16[32,2,288]{2,1,0:T(2,128)(2,1)S(1)}, u32[]{:S(2)}, u32[]{:S(2)}) async-start(bf16[32,2,288]{2,1,0:T(2,128)(2,1)} %reshape.59), calls=%async_computation.3 | async-start | bytes 98304 | tf_op jit(solution)/shard_map/all_to_all | solution.py:61
  322.2 0.0 all-reduce.5.cloned.1.call-start
  322.2 1.3 dynamic-slice.10
  323.5 1.3 dynamic-slice.8
  326.1 0.2 reshape.58
  326.2 1.0 convolution_bitcast_fusion.1
  327.2 0.0 all-reduce.5.cloned.1.call-update
  327.3 0.0 all-reduce.7.cloned.1.call-start
  327.3 18.7 %all-to-all-done.1 = bf16[32,2,288]{2,1,0:T(2,128)(2,1)S(1)} async-done(((bf16[32,2,288]{2,1,0:T(2,128)(2,1)}), bf16[32,2,288]{2,1,0:T(2,128)(2,1)S(1)}, u32[]{:S(2)}, u32[]{:S(2)}) %all-to-all-start.1) | async-done | bytes 36896 | tf_op jit(solution)/shard_map/all_to_all | solution.py:61
  346.0 0.2 reshape.60
  346.2 1.0 convolution_bitcast_fusion
  347.2 0.0 all-reduce.7.cloned.1.call-update
  347.2 241.7 %all-reduce.5.cloned.1.call-done = f32[1152,36]{0,1:T(8,128)} async-done(((f32[1152,36]{0,1:T(8,128)}), f32[1152,36]{0,1:T(8,128)}) %all-reduce.5.cloned.1.call-update) | async-done | bytes 165904
  588.9 0.9 constant_dynamic-slice_fusion.1
  589.7 0.7 copy.17
  590.4 162.7 %all-reduce.7.cloned.1.call-done = f32[1152,36]{0,1:T(8,128)} async-done(((f32[1152,36]{0,1:T(8,128)}), f32[1152,36]{0,1:T(8,128)}) %all-reduce.7.cloned.1.call-update) | async-done | bytes 165904
  753.1 0.9 constant_dynamic-slice_fusion
  754.0 0.7 copy.18
  (11 shorter events, 0.0 us)
Async XLA Ops:
  7.2 319.1 %copy-start = (bf16[512,1152]{1,0:T(8,128)(2,1)S(1)}, bf16[512,1152]{1,0:T(8,128)(2,1)}, u32[]{:S(2)}) copy-start(bf16[512,1152]{1,0:T(8,128)(2,1)} %param.9) | copy-start | bytes 3538948
  7.2 3.7 copy-start.1
  7.2 153.4 %reduce-scatter.5.cloned.1.call-start = ((), (), s32[]{:S(2)}) async-start(), calls=%async_computation.4 | async-start | bytes 2433024 | tf_op jit(solution)/shard_map/reduce_scatter | solution.py:32
  11.9 2.5 copy-start.4
  11.9 2.5 copy-start.5
  16.8 0.8 copy-start.2
  19.9 281.9 %reduce-scatter.7.cloned.1.call-start = ((), (), s32[]{:S(2)}) async-start(), calls=%async_computation.5 | async-start | bytes 2433024 | tf_op jit(solution)/shard_map/reduce_scatter | solution.py:48
  165.1 139.9 %all-to-all-start = ((bf16[32,2,288]{2,1,0:T(2,128)(2,1)}), bf16[32,2,288]{2,1,0:T(2,128)(2,1)S(1)}, u32[]{:S(2)}, u32[]{:S(2)}) async-start(bf16[32,2,288]{2,1,0:T(2,128)(2,1)} %reshape.57), calls=%async_computation.1 | async-start | bytes 98304 | tf_op jit(solution)/shard_map/all_to_all | solution.py:45
  304.2 42.0 %copy-start.3 = (bf16[512,1152]{1,0:T(8,128)(2,1)S(1)}, bf16[512,1152]{1,0:T(8,128)(2,1)}, u32[]{:S(2)}) copy-start(bf16[512,1152]{1,0:T(8,128)(2,1)} %param.10) | copy-start | bytes 3538948
  305.0 41.0 %all-to-all-start.1 = ((bf16[32,2,288]{2,1,0:T(2,128)(2,1)}), bf16[32,2,288]{2,1,0:T(2,128)(2,1)S(1)}, u32[]{:S(2)}, u32[]{:S(2)}) async-start(bf16[32,2,288]{2,1,0:T(2,128)(2,1)} %reshape.59), calls=%async_computation.3 | async-start | bytes 98304 | tf_op jit(solution)/shard_map/all_to_all | solution.py:61
  322.2 266.7 %all-reduce.5.cloned.1.call-start = ((), (), s32[]{:S(2)}) async-start(), calls=%async_computation.6 | async-start | bytes 368640
  327.3 425.9 %all-reduce.7.cloned.1.call-start = ((), (), s32[]{:S(2)}) async-start(), calls=%async_computation.7 | async-start | bytes 368640
Sparse Core Ops, SparseCore 0:
  20.0 140.5 reduce-scatter.4
  164.3 137.4 reduce-scatter.6
  327.4 261.4 all-reduce.4
  592.0 161.0 all-reduce.6
where the time goes:
time: 764 us; the launch traced here: 761 us
  waiting for transfers between devices  691 us (90%)
  starting transfers between devices  23 us (3%)
  between operations  16.6 us (2%)
  local copies, waits for them, and re-layouts  11.5 us (2%)
  matrix products  9.93 us (1%)
  other arithmetic  8.93 us (1%)
    unnamed x6, waiting for transfers between devices  404 us
    reduce_scatter x1, waiting for transfers between devices, per_device(): lax.psum_scatter(jnp.dot(sliced, txt_unit, preferred_element_type=jnp.flo...  137 us
    reduce_scatter x1, waiting for transfers between devices, per_device(): lax.psum_scatter(lax.dot_general(sliced, img_unit, (((0,), (0,)), ((), ()...  131 us
    all_to_all x1, waiting for transfers between devices, per_device(): lax.all_to_all(text_dz, 'dp', split_axis=1, concat_axis=0, tiled=True)  18.7 us
    all_to_all x1, starting transfers between devices, per_device(): lax.all_to_all(text_dz, 'dp', split_axis=1, concat_axis=0, tiled=True)  17.1 us
  transfers between devices with their start and end apart: 6, of which 5 were waited for; matrix products, arithmetic and copies ran while one was open for 2% of the time, Pallas kernels for 0%

commit v1 on v0

v1 whole, which is shorter than its diff:
```python
import functools

import jax
import jax.numpy as jnp
import numpy as np
from jax import lax
from jax.experimental import pallas as pl
from jax.experimental.pallas import tpu as pltpu
from jax.sharding import Mesh
from jax.sharding import PartitionSpec as P

F32 = jnp.float32
BF16 = jnp.bfloat16
TN = (((0,), (0,)), ((), ()))
NT = (((1,), (1,)), ((), ()))
VMEM_LIMIT = 56 * 1024 * 1024


def unit_rows(embedded):
    values = embedded.astype(F32)
    length = jnp.sqrt(jnp.sum(values * values, axis=1, keepdims=True) + 1e-06)
    inverse = 1.0 / length
    return (values * inverse).astype(BF16), inverse


def partial_kernel(
    n_chips,
    pad,
    pairs_total,
    core_ref,
    params_ref,
    img_ref,
    txt_ref,
    feats_ref,
    img_ids_ref,
    txt_ids_ref,
    mine_ref,
    other_ref,
    image_ref,
    text_ref,
):
    width = feats_ref.shape[1]
    block = width // (2 * n_chips)
    scale_t = params_ref[0]
    shift_b = params_ref[1]
    factor = scale_t * (-params_ref[2] / pairs_total)
    img_unit, img_inverse = unit_rows(img_ref[...])
    txt_unit, txt_inverse = unit_rows(txt_ref[...])
    similar = lax.dot_general(img_unit, txt_unit, NT, preferred_element_type=F32)
    logits = scale_t * similar + shift_b
    same = img_ids_ref[...] == txt_ids_ref[...]
    minus = jnp.where(same, logits, -logits)
    weights = (jnp.where(same, factor, -factor) / (1.0 + jnp.exp(minus))).astype(BF16)
    img_radial = jnp.sum(weights.astype(F32) * similar, axis=1, keepdims=True)
    img_grad = jnp.dot(weights, txt_unit, preferred_element_type=F32)
    img_grad = (img_grad - img_unit.astype(F32) * img_radial) * img_inverse
    image_ref[0:width, :] = img_grad.T
    txt_grad = lax.dot_general(weights, img_unit, TN, preferred_element_type=F32)
    txt_values = txt_unit.astype(F32)
    txt_radial = jnp.sum(txt_grad * txt_values, axis=1, keepdims=True)
    txt_grad = (txt_grad - txt_values * txt_radial) * txt_inverse
    high = txt_grad.astype(BF16)
    low = (txt_grad - high.astype(F32)).astype(BF16)
    feats = feats_ref[...]
    text_ref[0:width, :] = lax.dot_general(
        feats, high, TN, preferred_element_type=F32
    ) + lax.dot_general(feats, low, TN, preferred_element_type=F32)
    image_ref[width:, :] = jnp.zeros_like(image_ref[width:, :])
    text_ref[width:, :] = jnp.zeros_like(text_ref[width:, :])
    me = core_ref[0]
    for core in range(2):

        @pl.when(me == core)
        def _():
            for chip in range(n_chips):
                for kept, ref in ((core, mine_ref), (1 - core, other_ref)):
                    start = (2 * chip + kept) * block
                    ref[chip, :, 0:width] = text_ref[start : start + pad, :].astype(ref.dtype)
                    ref[chip, :, width:] = image_ref[start : start + pad, :].astype(ref.dtype)


def project_kernel(n_loop, block, parts_ref, feats_ref, out_ref, rows_ref):
    n_parts = parts_ref.shape[0]
    width = feats_ref.shape[1]
    total = parts_ref[0].astype(F32)
    for part in range(1, n_parts):
        total = total + parts_ref[part].astype(F32)
    text = total[0:block, 0:width]
    image = total[:, width:]
    high = image.astype(BF16)
    low = (image - high.astype(F32)).astype(BF16)
    feats = feats_ref[...]
    projected = jnp.dot(high, feats, preferred_element_type=F32) + jnp.dot(
        low, feats, preferred_element_type=F32
    )
    both = jnp.concatenate(
        [projected[0:block], text, jnp.zeros((128 - 2 * block, width), F32)], axis=0
    )
    rows_ref[...] = both.T
    first = out_ref.shape[1]
    rest = block - first
    lane = lax.broadcasted_iota(jnp.int32, (rest, 128), 1)
    for target in range(n_loop):
        top = rows_ref[target * block : target * block + first, :]
        bottom = rows_ref[target * block + first : (target + 1) * block, :]
        image_bottom = pltpu.roll(bottom, 2 * block, 1)
        text_bottom = pltpu.roll(bottom, block, 1)
        tail = jnp.concatenate([image_bottom, text_bottom], axis=0)
        lanes = lax.broadcasted_iota(jnp.int32, (first, 128), 1)
        out_ref[target] = jnp.where(lanes < 2 * block, top, tail).astype(out_ref.dtype)


def total_kernel(block, parts_ref, img_ref, txt_ref):
    total = parts_ref[0].astype(F32)
    for part in range(1, parts_ref.shape[0]):
        total = total + parts_ref[part].astype(F32)
    first = parts_ref.shape[1]
    rest = block - first
    image_bottom = pltpu.roll(total, 128 - 2 * block, 1)[0:rest]
    text_bottom = pltpu.roll(total, 128 - block, 1)[rest : 2 * rest]
    lane = lax.broadcasted_iota(jnp.int32, (rest, 128), 1)
    bottom = jnp.where(lane < block, image_bottom, text_bottom)
    whole = jnp.concatenate([total, bottom, jnp.zeros((128 - block, 128), F32)], axis=0)
    img_ref[...] = whole[0:block, 0:block]
    txt_ref[...] = whole.T[block : 2 * block, 0:block]


def whole_spec():
    return pl.BlockSpec(memory_space=pltpu.VMEM)


def scalar_spec():
    return pl.BlockSpec(memory_space=pltpu.SMEM)


def compiler_params():
    return pltpu.CompilerParams(vmem_limit_bytes=VMEM_LIMIT)


def per_device(img_embed, txt_embed, img_feats, txt_feats, img_ids, txt_ids, loss_params):
    n_loop = lax.axis_size("dp")
    n_chips = lax.axis_size(("dom", "chip"))
    rows, width = img_embed.shape
    block = width // n_loop
    pad = -(-block // 8) * 8
    core = lax.axis_index("core").astype(jnp.int32).reshape(1)
    lanes = width + rows
    shape = (n_chips, pad, lanes)
    mine, other = pl.pallas_call(
        functools.partial(partial_kernel, n_chips, pad, float(rows * n_loop)),
        out_shape=(jax.ShapeDtypeStruct(shape, F32), jax.ShapeDtypeStruct(shape, BF16)),
        in_specs=[scalar_spec(), scalar_spec()] + [whole_spec()] * 5,
        out_specs=[whole_spec()] * 2,
        scratch_shapes=[
            pltpu.VMEM((width + 8, rows), F32),
            pltpu.VMEM((width + 8, width), F32),
        ],
        compiler_params=compiler_params(),
        name="partial_gradients",
    )(
        core,
        loss_params,
        img_embed,
        txt_embed,
        txt_feats,
        img_ids.reshape(rows, 1),
        txt_ids.reshape(1, -1),
    )
    theirs = lax.ppermute(other, "core", [(0, 1), (1, 0)])
    chip_sum = (mine + theirs.astype(F32)).astype(BF16)
    parts = lax.all_to_all(chip_sum, ("dom", "chip"), split_axis=0, concat_axis=0, tiled=True)
    blocks = pl.pallas_call(
        functools.partial(project_kernel, n_loop, block),
        out_shape=jax.ShapeDtypeStruct((n_loop, 2 * block // 3, 128), BF16),
        in_specs=[whole_spec()] * 2,
        out_specs=whole_spec(),
        scratch_shapes=[pltpu.VMEM((width, 128), F32)],
        compiler_params=compiler_params(),
        name="project_blocks",
    )(parts, img_feats)
    loop_parts = lax.all_to_all(blocks, "dp", split_axis=0, concat_axis=0, tiled=True)
    return pl.pallas_call(
        functools.partial(total_kernel, block),
        out_shape=(jax.ShapeDtypeStruct((block, block), F32),) * 2,
        in_specs=[whole_spec()],
        out_specs=[whole_spec()] * 2,
        compiler_params=compiler_params(),
        name="sum_blocks",
    )(loop_parts)


def solution(mesh):
    shape = mesh.shape
    devices = np.asarray(mesh.devices).reshape(shape["dp"], shape["dom"], shape["mp"] // 2, 2)
    mesh = Mesh(devices, ("dp", "dom", "chip", "core"))
    plane = ("dom", "chip", "core")
    return jax.shard_map(
        per_device,
        mesh=mesh,
        in_specs=(
            P("dp", None),
            P(plane, None),
            P("dp", None),
            P(plane, None),
            P("dp"),
            P(plane),
            P(),
        ),
        out_specs=(P("dp", plane), P(plane, "dp")),
        check_vma=False,
    )
```

time: 764 us -> 128 us (0.17)
  waiting for transfers between devices: 691 us -> 4.38 us
  blocking collectives: 0 us -> 99.1 us
  starting transfers between devices: 23 us -> 1.91 us
  Pallas kernels: 0 us -> 16.9 us
  between operations: 16.6 us -> 0.65 us
  local copies, waits for them, and re-layouts: 11.5 us -> 1.52 us
  matrix products: 9.93 us -> 0 us
    unnamed x6 -> x0, waiting for transfers between devices: 404 us -> none
    reduce_scatter x2 -> x0, waiting for transfers between devices: 268 us -> none  [the longest x1 137 us: per_device(): lax.psum_scatter(jnp.dot(sliced, txt_unit, preferred_element_type=jnp.flo...]
    all_to_all x0 -> x2, blocking collectives: none -> 99.1 us  [the longest x1 55.4 us: per_device(): lax.all_to_all(blocks, 'dp', split_axis=0, concat_axis=0, tiled=True)]
    all_to_all x2 -> x0, starting transfers between devices: 22.8 us -> none  [the longest x1 17.1 us: per_device(): lax.all_to_all(text_dz, 'dp', split_axis=1, concat_axis=0, tiled=True)]
    all_to_all x2 -> x0, waiting for transfers between devices: 18.7 us -> none  [the longest x1 18.7 us: per_device(): lax.all_to_all(text_dz, 'dp', split_axis=1, concat_axis=0, tiled=True)]
    pallas_call x0 -> x3, Pallas kernels: none -> 16.9 us  [the longest x1 11.7 us: per_device(): pl.pallas_call(functools.partial(partial_kernel, n_chips, pad, float(rows...]
    dot_general x5 -> x0, matrix products: 9.93 us -> none  [the longest x1 3.32 us: per_device(): lax.dot_general(sliced, img_unit, (((0,), (0,)), ((), ())), preferred_ele...]
    unnamed x22 -> x0, local copies, waits for them, and re-layouts: 8.42 us -> none
  transfers between devices with their start and end apart: 6 -> 1, of which waited for: 5 -> 1; matrix products, arithmetic and copies ran while one was open for 2% -> 0% of each run, Pallas kernels for 0% -> 0%
where the time goes in v1:
time: 128 us; the launch traced here: 127 us
  blocking collectives  99.1 us (77%)
  Pallas kernels  16.9 us (13%)
  waiting for transfers between devices  4.38 us (3%)
  other arithmetic  2.7 us (2%)
  starting transfers between devices  1.91 us (1%)
  local copies, waits for them, and re-layouts  1.52 us (1%)
    all_to_all x1, blocking collectives, per_device(): lax.all_to_all(blocks, 'dp', split_axis=0, concat_axis=0, tiled=True)  55.4 us
    all_to_all x1, blocking collectives, per_device(): lax.all_to_all(chip_sum, ('dom', 'chip'), split_axis=0, concat_axis=0, ti...  43.7 us
    pallas_call x1, Pallas kernels, per_device(): pl.pallas_call(functools.partial(partial_kernel, n_chips, pad, float(rows...  11.7 us
    ppermute x1, waiting for transfers between devices, per_device(): theirs = lax.ppermute(other, 'core', [(0, 1), (1, 0)])  4.38 us
    pallas_call x1, Pallas kernels, per_device(): pl.pallas_call(functools.partial(project_kernel, n_loop, block), out_shap...  3.48 us
    convert_element_type x1, other arithmetic, per_device(): chip_sum = (mine + theirs.astype(F32)).astype(BF16)  2.7 us
  transfers between devices with their start and end apart: 1, of which 1 were waited for; matrix products, arithmetic and copies ran while one was open for 0% of the time, Pallas kernels for 0%

profile of v1, /device:TPU:6, one launch (start us, length us, event | category | flops | bytes accessed | tf_op | source)
XLA Modules:
  0.0 127.2 jit_solution(15756948922119371834)
XLA Ops:
  0.6 1.5 %copy.9.img_ids_ref = s32[512,1]{1,0:T(8,128)} copy(s32[512,1]{0,1:T(1,128)} %bitcast.3) | data formatting | bytes 4096 | tf_op jit(solution)/shard_map/reshape | solution.py:166
  2.2 11.7 %partial_gradients.1 = (f32[16,40,1664]{2,1,0:T(8,128)}, bf16[16,40,1664]{2,1,0:T(8,128)(2,1)}) custom-call(s32[1]{0:T(128)} %bitcast.core_ref, f32[3]{0:T(128)} %params_ref.1, bf16[512,1152]{1,0:T(8,128)(2,1)} %img_ref.1, bf16[512,1152]{1,0:T(8,128)(2,1)} %txt_ref.1, bf16[512,1152]{1,0:T(8,128)(2,1)} %feats_ref.2, s32[512,1]{1,0:T(8,128)} %copy.9.img_ids_ref, ...), custom_call_target="tpu_custom_call" | custom-call | tf_op jit(solution)/shard_map/partial_gradients/pallas_call | solution.py:149
  13.9 1.9 %collective-permute-start = (bf16[16,40,1664]{2,1,0:T(8,128)(2,1)}, bf16[16,40,1664]{2,1,0:T(8,128)(2,1)S(1)}, u32[]{:S(2)}, u32[]{:S(2)}) collective-permute-start(bf16[16,40,1664]{2,1,0:T(8,128)(2,1)} %get-tuple-element.5), channel_id=1, source_target_pairs={{0,1},{1,0},{2,3},{3,2},{4,5},{5,4},{6,7},{7,6},{8,9},{9,8},{10,11... | collective-permute-start | bytes 6389768 | tf_op jit(solution)/shard_map/ppermute | solution.py:169
  15.8 4.4 %collective-permute-done = bf16[16,40,1664]{2,1,0:T(8,128)(2,1)S(1)} collective-permute-done((bf16[16,40,1664]{2,1,0:T(8,128)(2,1)}, bf16[16,40,1664]{2,1,0:T(8,128)(2,1)S(1)}, u32[]{:S(2)}, u32[]{:S(2)}) %collective-permute-start) | collective-permute-done | bytes 2129952 | tf_op jit(solution)/shard_map/ppermute | solution.py:169
  20.2 2.7 %add_convert_fusion = bf16[16,40,1664]{2,1,0:T(8,128)(2,1)S(1)} fusion(f32[16,40,1664]{2,1,0:T(8,128)} %get-tuple-element.4, bf16[16,40,1664]{2,1,0:T(8,128)(2,1)S(1)} %collective-permute-done), kind=kLoop, calls=%fused_computation | loop fusion | flops 3194880 | bytes 8519680 | tf_op jit(solution)/shard_map/convert_element_type | solution.py:170
  22.9 43.7 %all_to_all.10.parts_ref = bf16[16,40,1664]{2,1,0:T(8,128)(2,1)} all-to-all(bf16[16,40,1664]{2,1,0:T(8,128)(2,1)S(1)} %add_convert_fusion), channel_id=1, replica_groups=mesh['dp'=32,'dom'=2,'chip'=8,'core'=2] {'dom','chip'}, dimensions={0} | all-to-all | bytes 4259840 | tf_op jit(solution)/shard_map/all_to_all | solution.py:171
  66.6 3.5 %project_blocks.1 = bf16[32,24,128]{2,1,0:T(8,128)(2,1)} custom-call(bf16[16,40,1664]{2,1,0:T(8,128)(2,1)} %all_to_all.10.parts_ref, bf16[512,1152]{1,0:T(8,128)(2,1)} %feats_ref.3), custom_call_target="tpu_custom_call" | custom-call | tf_op jit(solution)/shard_map/project_blocks/pallas_call | solution.py:172
  70.1 55.4 %all_to_all.11.parts_ref = bf16[32,24,128]{2,1,0:T(8,128)(2,1)} all-to-all(bf16[32,24,128]{2,1,0:T(8,128)(2,1)} %project_blocks.1), channel_id=1, replica_groups=mesh['dp'=32,'dom'=2,'chip'=8,'core'=2] {'dp'}, dimensions={0} | all-to-all | bytes 393216 | tf_op jit(solution)/shard_map/all_to_all | solution.py:181
  125.5 1.7 %sum_blocks.1 = (f32[36,36]{1,0:T(8,128)}, f32[36,36]{1,0:T(8,128)}) custom-call(bf16[32,24,128]{2,1,0:T(8,128)(2,1)} %all_to_all.11.parts_ref), custom_call_target="tpu_custom_call" | custom-call | tf_op jit(solution)/shard_map/sum_blocks/pallas_call | solution.py:182
Async XLA Ops:
  13.9 6.3 %collective-permute-start = (bf16[16,40,1664]{2,1,0:T(8,128)(2,1)}, bf16[16,40,1664]{2,1,0:T(8,128)(2,1)S(1)}, u32[]{:S(2)}, u32[]{:S(2)}) collective-permute-start(bf16[16,40,1664]{2,1,0:T(8,128)(2,1)} %get-tuple-element.5), channel_id=1, source_target_pairs={{0,1},{1,0},{2,3},{3,2},{4,5},{5,4},{6,7},{7,6},{8,9},{9,8},{10,11... | collective-permute-start | bytes 6389768 | tf_op jit(solution)/shard_map/ppermute | solution.py:169

commit v2 on v1

v2 whole, which is shorter than its diff:
```python
import functools

import jax
import jax.numpy as jnp
import numpy as np
from jax import lax
from jax.experimental import pallas as pl
from jax.experimental.pallas import tpu as pltpu
from jax.sharding import Mesh
from jax.sharding import PartitionSpec as P

F32 = jnp.float32
BF16 = jnp.bfloat16
TN = (((0,), (0,)), ((), ()))
NT = (((1,), (1,)), ((), ()))


def unit_rows(embedded):
    values = embedded.astype(F32)
    length = jnp.sqrt(jnp.sum(values * values, axis=1, keepdims=True) + 1e-06)
    inverse = 1.0 / length
    return (values * inverse).astype(BF16), inverse


def partial_kernel(
    n_chips,
    pairs_total,
    core_ref,
    params_hbm,
    img_hbm,
    txt_hbm,
    feats_hbm,
    img_ids_hbm,
    txt_ids_hbm,
    mine_ref,
    other_ref,
    grads_ref,
    params_ref,
    img_ref,
    txt_ref,
    feats_ref,
    img_ids_ref,
    txt_ids_ref,
    sems,
):
    copies = []
    for number, (source, target) in enumerate(
        (
            (img_hbm, img_ref),
            (txt_hbm, txt_ref),
            (img_ids_hbm, img_ids_ref),
            (txt_ids_hbm, txt_ids_ref),
            (params_hbm, params_ref),
            (feats_hbm, feats_ref),
        )
    ):
        copies.append(pltpu.make_async_copy(source, target, sems.at[number]))
        copies[-1].start()
    rows = img_ref.shape[0]
    width = feats_ref.shape[1]
    pair = width // n_chips
    block = pair // 2
    body = block // 8 * 8
    n_tiles = (width + rows) // 128
    copies[0].wait()
    img_unit, img_inverse = unit_rows(img_ref[...])
    copies[1].wait()
    txt_unit, txt_inverse = unit_rows(txt_ref[...])
    for copy in copies[2:5]:
        copy.wait()
    scale_t = params_ref[0]
    shift_b = params_ref[1]
    factor = scale_t * (-params_ref[2] / pairs_total)
    similar = lax.dot_general(img_unit, txt_unit, NT, preferred_element_type=F32)
    logits = scale_t * similar + shift_b
    img_ids = jnp.broadcast_to(img_ids_ref[...], (8, rows)).T[:, 0:1]
    same = img_ids == txt_ids_ref[...]
    minus = jnp.where(same, logits, -logits)
    weights = (jnp.where(same, factor, -factor) / (1.0 + jnp.exp(minus))).astype(BF16)
    img_radial = jnp.sum(weights.astype(F32) * similar, axis=1, keepdims=True)
    img_grad = jnp.dot(weights, txt_unit, preferred_element_type=F32)
    img_grad = (img_grad - img_unit.astype(F32) * img_radial) * img_inverse
    grads_ref[:, width:] = img_grad.T
    txt_grad = lax.dot_general(weights, img_unit, TN, preferred_element_type=F32)
    txt_values = txt_unit.astype(F32)
    txt_radial = jnp.sum(txt_grad * txt_values, axis=1, keepdims=True)
    txt_grad = ((txt_grad - txt_values * txt_radial) * txt_inverse).astype(BF16)
    copies[5].wait()
    grads_ref[:, 0:width] = lax.dot_general(
        feats_ref[...], txt_grad, TN, preferred_element_type=F32
    )
    me = core_ref[0]
    low_half = lax.broadcasted_iota(jnp.int32, (8, 128), 0) < 4
    for core in range(2):

        @pl.when(me == core)
        def _():
            for chip in range(n_chips):
                shared = grads_ref[pair * chip + body : pair * chip + body + 8, :]
                turned = pltpu.roll(shared, 4, 0)
                for kept, ref in ((core, mine_ref), (1 - core, other_ref)):
                    start = pair * chip + (body + 8) * kept
                    whole = grads_ref[start : start + body, :].astype(ref.dtype)
                    even, odd = (turned, shared) if kept else (shared, turned)
                    for tile in range(n_tiles):
                        ref[chip, body * tile : body * (tile + 1), :] = whole[
                            :, 128 * tile : 128 * (tile + 1)
                        ]
                    ends = []
                    for tile in range(0, n_tiles, 2):
                        last = min(tile + 1, n_tiles - 1)
                        ends.append(
                            jnp.where(
                                low_half,
                                even[:, 128 * tile : 128 * (tile + 1)],
                                odd[:, 128 * last : 128 * (last + 1)],
                            )
                        )
                    ref[chip, body * n_tiles :, :] = jnp.concatenate(ends, axis=0).astype(ref.dtype)


def project_kernel(n_loop, block, parts_ref, feats_ref, out_ref, rows_ref, total_ref):
    n_parts = parts_ref.shape[0]
    rows, width = feats_ref.shape
    body = block // 8 * 8
    n_tiles = (width + rows) // 128
    total = parts_ref[0].astype(F32)
    for part in range(1, n_parts):
        total = total + parts_ref[part].astype(F32)
    for tile in range(n_tiles):
        columns = slice(128 * tile, 128 * (tile + 1))
        total_ref[0:body, columns] = total[body * tile : body * (tile + 1)]
        start = body * n_tiles + 8 * (tile // 2)
        end = total[start : start + 8]
        total_ref[body : body + 8, columns] = pltpu.roll(end, 4, 0) if tile % 2 else end
    text = total_ref[0:block, 0:width]
    image = total_ref[:, width:]
    high = image.astype(BF16)
    low = (image - high.astype(F32)).astype(BF16)
    feats = feats_ref[...]
    projected = jnp.dot(high, feats, preferred_element_type=F32) + jnp.dot(
        low, feats, preferred_element_type=F32
    )
    both = jnp.concatenate(
        [projected[0:block], text, jnp.zeros((128 - 2 * block, width), F32)], axis=0
    )
    rows_ref[...] = both.T
    first = out_ref.shape[1]
    rest = block - first
    lane = lax.broadcasted_iota(jnp.int32, (first, 128), 1)
    for target in range(n_loop):
        top = rows_ref[target * block : target * block + first, :]
        bottom = rows_ref[target * block + first : (target + 1) * block, :]
        tail = jnp.concatenate(
            [pltpu.roll(bottom, 2 * block, 1), pltpu.roll(bottom, block, 1)], axis=0
        )
        out_ref[target] = jnp.where(lane < 2 * block, top, tail).astype(out_ref.dtype)


def total_kernel(block, core_ref, parts_ref, img_ref, txt_ref):
    total = parts_ref[0].astype(F32)
    for part in range(1, parts_ref.shape[0]):
        total = total + parts_ref[part].astype(F32)
    first = parts_ref.shape[1]
    rest = block - first
    extra = block % 8
    image_bottom = pltpu.roll(total, 128 - 2 * block, 1)[0:rest]
    text_bottom = pltpu.roll(total, 128 - block, 1)[rest : 2 * rest]
    lane = lax.broadcasted_iota(jnp.int32, (rest, 128), 1)
    bottom = jnp.where(lane < block, image_bottom, text_bottom)
    whole = jnp.concatenate([total, bottom, jnp.zeros((128 - block, 128), F32)], axis=0)
    place = lax.broadcasted_iota(jnp.int32, whole.shape, 1)
    inside = jnp.where(place < block, place, place - block)
    ordered = jnp.where(
        inside < extra, pltpu.roll(whole, 128 - (block - extra), 1), pltpu.roll(whole, extra, 1)
    )
    whole = jnp.where(core_ref[0] == 1, ordered, whole)
    img_ref[...] = whole[0:block, 0:block]
    txt_ref[...] = whole.T[block : 2 * block, 0:block]


def whole_spec():
    return pl.BlockSpec(memory_space=pltpu.VMEM)


def scalar_spec():
    return pl.BlockSpec(memory_space=pltpu.SMEM)


def compiler_params(mib):
    return pltpu.CompilerParams(vmem_limit_bytes=mib * 1024 * 1024)


def per_device(img_embed, txt_embed, img_feats, txt_feats, img_ids, txt_ids, loss_params):
    n_loop = lax.axis_size("dp")
    n_chips = lax.axis_size(("dom", "chip"))
    rows, width = img_embed.shape
    block = width // n_loop
    core = lax.axis_index("core").astype(jnp.int32).reshape(1)
    lanes = width + rows
    shape = (n_chips, -(-block * (lanes // 128) // 8) * 8, 128)
    mine, other = pl.pallas_call(
        functools.partial(partial_kernel, n_chips, float(rows * n_loop)),
        out_shape=(jax.ShapeDtypeStruct(shape, F32), jax.ShapeDtypeStruct(shape, BF16)),
        in_specs=[scalar_spec()] + [pl.BlockSpec(memory_space=pltpu.HBM)] * 6,
        out_specs=[whole_spec()] * 2,
        scratch_shapes=[
            pltpu.VMEM((width, lanes), F32),
            pltpu.SMEM(loss_params.shape, F32),
            pltpu.VMEM(img_embed.shape, BF16),
            pltpu.VMEM(txt_embed.shape, BF16),
            pltpu.VMEM(txt_feats.shape, BF16),
            pltpu.VMEM((1, rows), jnp.int32),
            pltpu.VMEM((1, txt_ids.shape[0]), jnp.int32),
            pltpu.SemaphoreType.DMA((6,)),
        ],
        compiler_params=compiler_params(36),
        name="partial_gradients",
    )(
        core,
        *(
            pltpu.with_memory_space_constraint(array, pltpu.HBM)
            for array in (
                loss_params,
                img_embed,
                txt_embed,
                txt_feats,
                img_ids.reshape(1, rows),
                txt_ids.reshape(1, -1),
            )
        ),
    )
    theirs = lax.ppermute(other, "core", [(0, 1), (1, 0)])
    chip_sum = (mine + theirs.astype(F32)).astype(BF16)
    parts = lax.all_to_all(chip_sum, ("dom", "chip"), split_axis=0, concat_axis=0, tiled=True)
    blocks = pl.pallas_call(
        functools.partial(project_kernel, n_loop, block),
        out_shape=jax.ShapeDtypeStruct((n_loop, 2 * block // 3, 128), BF16),
        in_specs=[whole_spec()] * 2,
        out_specs=whole_spec(),
        scratch_shapes=[
            pltpu.VMEM((width, 128), F32),
            pltpu.VMEM((block // 8 * 8 + 8, lanes), F32),
        ],
        compiler_params=compiler_params(16),
        name="project_blocks",
    )(parts, img_feats)
    loop_parts = lax.all_to_all(blocks, "dp", split_axis=0, concat_axis=0, tiled=True)
    return pl.pallas_call(
        functools.partial(total_kernel, block),
        out_shape=(jax.ShapeDtypeStruct((block, block), F32),) * 2,
        in_specs=[scalar_spec(), whole_spec()],
        out_specs=[whole_spec()] * 2,
        compiler_params=compiler_params(4),
        name="sum_blocks",
    )(core, loop_parts)


def solution(mesh):
    shape = mesh.shape
    devices = np.asarray(mesh.devices).reshape(shape["dp"], shape["dom"], shape["mp"] // 2, 2)
    mesh = Mesh(devices, ("dp", "dom", "chip", "core"))
    plane = ("dom", "chip", "core")
    return jax.shard_map(
        per_device,
        mesh=mesh,
        in_specs=(
            P("dp", None),
            P(plane, None),
            P("dp", None),
            P(plane, None),
            P("dp"),
            P(plane),
            P(),
        ),
        out_specs=(P("dp", plane), P(plane, "dp")),
        check_vma=False,
    )
```

time: 128 us -> 113 us (0.88)
  Pallas kernels: 16.9 us -> 9.06 us
  blocking collectives: 99.1 us -> 96.6 us
  other arithmetic: 2.7 us -> 0.45 us
  local copies, waits for them, and re-layouts: 1.52 us -> 0.01 us
    pallas_call x1, Pallas kernels: 11.7 us -> 7.29 us  [per_device(): pl.pallas_call(functools.partial(partial_kernel, n_chips, float(rows * n_...]
    all_to_all x1, blocking collectives: 43.7 us -> 40.8 us  [per_device(): lax.all_to_all(chip_sum, ('dom', 'chip'), split_axis=0, concat_axis=0, ti...]
    pallas_call x1, Pallas kernels: 3.48 us -> 0.9 us  [per_device(): pl.pallas_call(functools.partial(project_kernel, n_loop, block), out_shap...]
    convert_element_type x1, other arithmetic: 2.7 us -> 0.45 us  [per_device(): chip_sum = (mine + theirs.astype(F32)).astype(BF16)]
    reshape x1 -> x0, local copies, waits for them, and re-layouts: 1.52 us -> none  [per_device(): img_ids.reshape(rows, 1)]
where the time goes in v2:
time: 113 us
  blocking collectives  96.6 us (85%)
  Pallas kernels  9.06 us (8%)
  waiting for transfers between devices  3.89 us (3%)
  starting transfers between devices  1.92 us (2%)
    all_to_all x1, blocking collectives, per_device(): lax.all_to_all(blocks, 'dp', split_axis=0, concat_axis=0, tiled=True)  55.8 us
    all_to_all x1, blocking collectives, per_device(): lax.all_to_all(chip_sum, ('dom', 'chip'), split_axis=0, concat_axis=0, ti...  40.8 us
    pallas_call x1, Pallas kernels, per_device(): pl.pallas_call(functools.partial(partial_kernel, n_chips, float(rows * n_...  7.29 us
    ppermute x1, waiting for transfers between devices, per_device(): theirs = lax.ppermute(other, 'core', [(0, 1), (1, 0)])  3.89 us
  transfers between devices with their start and end apart: 1, of which 1 were waited for; matrix products, arithmetic and copies ran while one was open for 0% of the time, Pallas kernels for 0%

profile of v2, /device:TPU:6, one launch (start us, length us, event | category | flops | bytes accessed | tf_op | source)
XLA Modules:
  0.0 112.6 jit_solution(3644529332003475291)
XLA Ops:
  0.6 7.3 %partial_gradients.1 = (f32[16,472,128]{2,1,0:T(8,128)S(1)}, bf16[16,472,128]{2,1,0:T(8,128)(2,1)S(1)}) custom-call(s32[1]{0:T(128)} %bitcast.core_ref, f32[3]{0:T(128)} %params_hbm.1, bf16[512,1152]{1,0:T(8,128)(2,1)} %img_hbm.1, bf16[512,1152]{1,0:T(8,128)(2,1)} %txt_hbm.1, bf16[512,1152]{1,0:T(8,128)(2,1)} %feats_hbm.1, s32[1,512]{1,0:T(1,128)} %bitcast.3, ...), custom_call_target="tpu_custom_call" | custom-call | tf_op jit(solution)/shard_map/partial_gradients/pallas_call | solution.py:202
  7.9 1.9 %collective-permute-start = (bf16[16,472,128]{2,1,0:T(8,128)(2,1)S(1)}, bf16[16,472,128]{2,1,0:T(8,128)(2,1)S(1)}, u32[]{:S(2)}, u32[]{:S(2)}) collective-permute-start(bf16[16,472,128]{2,1,0:T(8,128)(2,1)S(1)} %get-tuple-element.5), channel_id=1, source_target_pairs={{0,1},{1,0},{2,3},{3,2},{4,5},{5,4},{6,7},{7,6},{8,9},{9,8},{10,11... | collective-permute-start | bytes 5799944 | tf_op jit(solution)/shard_map/ppermute | solution.py:233
  9.9 3.9 %collective-permute-done = bf16[16,472,128]{2,1,0:T(8,128)(2,1)S(1)} collective-permute-done((bf16[16,472,128]{2,1,0:T(8,128)(2,1)S(1)}, bf16[16,472,128]{2,1,0:T(8,128)(2,1)S(1)}, u32[]{:S(2)}, u32[]{:S(2)}) %collective-permute-start) | collective-permute-done | bytes 1933344 | tf_op jit(solution)/shard_map/ppermute | solution.py:233
  13.8 0.5 add_convert_fusion
  14.2 0.0 copy-start
  14.2 40.8 %all_to_all.10.parts_ref = bf16[16,472,128]{2,1,0:T(8,128)(2,1)S(1)} all-to-all(bf16[16,472,128]{2,1,0:T(8,128)(2,1)S(1)} %add_convert_fusion), channel_id=1, replica_groups=mesh['dp'=32,'dom'=2,'chip'=8,'core'=2] {'dom','chip'}, dimensions={0} | all-to-all | bytes 3866624 | tf_op jit(solution)/shard_map/all_to_all | solution.py:235
  55.0 0.0 copy-done
  55.0 0.9 project_blocks.1
  55.9 55.8 %all_to_all.11.parts_ref = bf16[32,24,128]{2,1,0:T(8,128)(2,1)S(1)} all-to-all(bf16[32,24,128]{2,1,0:T(8,128)(2,1)S(1)} %project_blocks.1), channel_id=1, replica_groups=mesh['dp'=32,'dom'=2,'chip'=8,'core'=2] {'dp'}, dimensions={0} | all-to-all | bytes 393216 | tf_op jit(solution)/shard_map/all_to_all | solution.py:248
  111.7 0.9 sum_blocks.1
Async XLA Ops:
  7.9 5.8 %collective-permute-start = (bf16[16,472,128]{2,1,0:T(8,128)(2,1)S(1)}, bf16[16,472,128]{2,1,0:T(8,128)(2,1)S(1)}, u32[]{:S(2)}, u32[]{:S(2)}) collective-permute-start(bf16[16,472,128]{2,1,0:T(8,128)(2,1)S(1)} %get-tuple-element.5), channel_id=1, source_target_pairs={{0,1},{1,0},{2,3},{3,2},{4,5},{5,4},{6,7},{7,6},{8,9},{9,8},{10,11... | collective-permute-start | bytes 5799944 | tf_op jit(solution)/shard_map/ppermute | solution.py:233
  14.2 40.8 %copy-start = (bf16[512,1152]{1,0:T(8,128)(2,1)S(1)}, bf16[512,1152]{1,0:T(8,128)(2,1)}, u32[]{:S(2)}) copy-start(bf16[512,1152]{1,0:T(8,128)(2,1)} %feats_ref.1) | copy-start | bytes 3538948

commit v3 on v2

--- a/solution.py
+++ b/solution.py
@@ -24,8 +24,9 @@
 
 def partial_kernel(
     n_chips,
+    first_chip,
     pairs_total,
-    core_ref,
+    place_ref,
     params_hbm,
     img_hbm,
     txt_hbm,
@@ -89,7 +90,7 @@
     grads_ref[:, 0:width] = lax.dot_general(
         feats_ref[...], txt_grad, TN, preferred_element_type=F32
     )
-    me = core_ref[0]
+    me = place_ref[0] % 2
     low_half = lax.broadcasted_iota(jnp.int32, (8, 128), 0) < 4
     for core in range(2):
 
@@ -98,12 +99,13 @@
             for chip in range(n_chips):
                 shared = grads_ref[pair * chip + body : pair * chip + body + 8, :]
                 turned = pltpu.roll(shared, 4, 0)
+                slot = (chip - first_chip) % n_chips
                 for kept, ref in ((core, mine_ref), (1 - core, other_ref)):
                     start = pair * chip + (body + 8) * kept
                     whole = grads_ref[start : start + body, :].astype(ref.dtype)
                     even, odd = (turned, shared) if kept else (shared, turned)
                     for tile in range(n_tiles):
-                        ref[chip, body * tile : body * (tile + 1), :] = whole[
+                        ref[slot, body * tile : body * (tile + 1), :] = whole[
                             :, 128 * tile : 128 * (tile + 1)
                         ]
                     ends = []
@@ -116,10 +118,21 @@
                                 odd[:, 128 * last : 128 * (last + 1)],
                             )
                         )
-                    ref[chip, body * n_tiles :, :] = jnp.concatenate(ends, axis=0).astype(ref.dtype)
-
-
-def project_kernel(n_loop, block, parts_ref, feats_ref, out_ref, rows_ref, total_ref):
+                    ref[slot, body * n_tiles :, :] = jnp.concatenate(ends, axis=0).astype(ref.dtype)
+
+
+def project_kernel(
+    first_far,
+    block,
+    place_ref,
+    parts_ref,
+    feats_ref,
+    mine_ref,
+    other_ref,
+    rows_ref,
+    total_ref,
+    blocks_ref,
+):
     n_parts = parts_ref.shape[0]
     rows, width = feats_ref.shape
     body = block // 8 * 8
@@ -145,19 +158,24 @@
         [projected[0:block], text, jnp.zeros((128 - 2 * block, width), F32)], axis=0
     )
     rows_ref[...] = both.T
-    first = out_ref.shape[1]
+    first = mine_ref.shape[1]
+    n_near, n_far = blocks_ref.shape[0:2]
     rest = block - first
     lane = lax.broadcasted_iota(jnp.int32, (first, 128), 1)
-    for target in range(n_loop):
+    for target in range(n_far * n_near):
         top = rows_ref[target * block : target * block + first, :]
         bottom = rows_ref[target * block + first : (target + 1) * block, :]
         tail = jnp.concatenate(
             [pltpu.roll(bottom, 2 * block, 1), pltpu.roll(bottom, block, 1)], axis=0
         )
-        out_ref[target] = jnp.where(lane < 2 * block, top, tail).astype(out_ref.dtype)
-
-
-def total_kernel(block, core_ref, parts_ref, img_ref, txt_ref):
+        place = (target // n_near - first_far) % n_far
+        blocks_ref[target % n_near, place] = jnp.where(lane < 2 * block, top, tail)
+    near = place_ref[0] // 2
+    mine_ref[...] = blocks_ref[near]
+    other_ref[...] = blocks_ref[1 - near].astype(other_ref.dtype)
+
+
+def total_kernel(block, place_ref, parts_ref, img_ref, txt_ref):
     total = parts_ref[0].astype(F32)
     for part in range(1, parts_ref.shape[0]):
         total = total + parts_ref[part].astype(F32)
@@ -174,7 +192,7 @@
     ordered = jnp.where(
         inside < extra, pltpu.roll(whole, 128 - (block - extra), 1), pltpu.roll(whole, extra, 1)
     )
-    whole = jnp.where(core_ref[0] == 1, ordered, whole)
+    whole = jnp.where(place_ref[0] % 2 == 1, ordered, whole)
     img_ref[...] = whole[0:block, 0:block]
     txt_ref[...] = whole.T[block : 2 * block, 0:block]
 
@@ -191,16 +209,22 @@
     return pltpu.CompilerParams(vmem_limit_bytes=mib * 1024 * 1024)
 
 
+def turned(size, first):
+    return [(first + number) % size for number in range(size)]
+
+
 def per_device(img_embed, txt_embed, img_feats, txt_feats, img_ids, txt_ids, loss_params):
-    n_loop = lax.axis_size("dp")
-    n_chips = lax.axis_size(("dom", "chip"))
+    n_far, n_near = lax.axis_size("far"), lax.axis_size("near")
+    n_loop = n_far * n_near
+    n_chips = lax.axis_size("chip")
     rows, width = img_embed.shape
     block = width // n_loop
-    core = lax.axis_index("core").astype(jnp.int32).reshape(1)
+    first_chip = n_chips // 2 + n_chips // 8
+    place = lax.axis_index(("near", "core")).astype(jnp.int32).reshape(1)
     lanes = width + rows
     shape = (n_chips, -(-block * (lanes // 128) // 8) * 8, 128)
     mine, other = pl.pallas_call(
-        functools.partial(partial_kernel, n_chips, float(rows * n_loop)),
+        functools.partial(partial_kernel, n_chips, first_chip, float(rows * n_loop)),
         out_shape=(jax.ShapeDtypeStruct(shape, F32), jax.ShapeDtypeStruct(shape, BF16)),
         in_specs=[scalar_spec()] + [pl.BlockSpec(memory_space=pltpu.HBM)] * 6,
         out_specs=[whole_spec()] * 2,
@@ -217,7 +241,7 @@
         compiler_params=compiler_params(36),
         name="partial_gradients",
     )(
-        core,
+        place,
         *(
             pltpu.with_memory_space_constraint(array, pltpu.HBM)
             for array in (
@@ -232,20 +256,34 @@
     )
     theirs = lax.ppermute(other, "core", [(0, 1), (1, 0)])
     chip_sum = (mine + theirs.astype(F32)).astype(BF16)
-    parts = lax.all_to_all(chip_sum, ("dom", "chip"), split_axis=0, concat_axis=0, tiled=True)
-    blocks = pl.pallas_call(
-        functools.partial(project_kernel, n_loop, block),
-        out_shape=jax.ShapeDtypeStruct((n_loop, 2 * block // 3, 128), BF16),
-        in_specs=[whole_spec()] * 2,
-        out_specs=whole_spec(),
+    parts = lax.all_to_all(
+        chip_sum,
+        "chip",
+        split_axis=0,
+        concat_axis=0,
+        axis_index_groups=[turned(n_chips, first_chip)],
+        tiled=True,
+    )
+    first_far = n_far // 2
+    shape = (n_far, 2 * block // 3, 128)
+    mine, other = pl.pallas_call(
+        functools.partial(project_kernel, first_far, block),
+        out_shape=(jax.ShapeDtypeStruct(shape, F32), jax.ShapeDtypeStruct(shape, BF16)),
+        in_specs=[scalar_spec()] + [whole_spec()] * 2,
+        out_specs=[whole_spec()] * 2,
         scratch_shapes=[
             pltpu.VMEM((width, 128), F32),
             pltpu.VMEM((block // 8 * 8 + 8, lanes), F32),
+            pltpu.VMEM((n_near,) + shape, F32),
         ],
         compiler_params=compiler_params(16),
         name="project_blocks",
-    )(parts, img_feats)
-    loop_parts = lax.all_to_all(blocks, "dp", split_axis=0, concat_axis=0, tiled=True)
+    )(place, parts, img_feats)
+    theirs = lax.ppermute(other, "near", [(0, 1), (1, 0)])
+    near_sum = (mine + theirs.astype(F32)).astype(BF16)
+    loop_parts = lax.all_to_all(
+        near_sum, "far", split_axis=0, concat_axis=0, axis_index_groups=[turned(n_far, first_far)], tiled=True
+    )
     return pl.pallas_call(
         functools.partial(total_kernel, block),
         out_shape=(jax.ShapeDtypeStruct((block, block), F32),) * 2,
@@ -253,26 +291,28 @@
         out_specs=[whole_spec()] * 2,
         compiler_params=compiler_params(4),
         name="sum_blocks",
-    )(core, loop_parts)
+    )(place, loop_parts)
 
 
 def solution(mesh):
     shape = mesh.shape
-    devices = np.asarray(mesh.devices).reshape(shape["dp"], shape["dom"], shape["mp"] // 2, 2)
-    mesh = Mesh(devices, ("dp", "dom", "chip", "core"))
-    plane = ("dom", "chip", "core")
+    near = 2
+    sizes = (shape["dp"] // near, near, shape["dom"] * shape["mp"] // 2, 2)
+    mesh = Mesh(np.asarray(mesh.devices).reshape(sizes), ("far", "near", "chip", "core"))
+    loop = ("far", "near")
+    plane = ("chip", "core")
     return jax.shard_map(
         per_device,
         mesh=mesh,
         in_specs=(
-            P("dp", None),
+            P(loop, None),
             P(plane, None),
-            P("dp", None),
+            P(loop, None),
             P(plane, None),
-            P("dp"),
+            P(loop),
             P(plane),
             P(),
         ),
-        out_specs=(P("dp", plane), P(plane, "dp")),
+        out_specs=(P(loop, plane), P(plane, loop)),
         check_vma=False,
     )

time: 113 us -> 95.8 us (0.85)
  blocking collectives: 96.6 us -> 71.9 us
  waiting for transfers between devices: 3.89 us -> 8.47 us
  starting transfers between devices: 1.92 us -> 3.84 us
    all_to_all x2, blocking collectives: 96.6 us -> 71.9 us  [the longest x1 40.8 us: per_device(): lax.all_to_all(chip_sum, 'chip', split_axis=0, concat_axis=0, axis_index_...]
    ppermute x0 -> x1, waiting for transfers between devices: none -> 4.58 us  [per_device(): theirs = lax.ppermute(other, 'near', [(0, 1), (1, 0)])]
    ppermute x0 -> x1, starting transfers between devices: none -> 1.92 us  [per_device(): theirs = lax.ppermute(other, 'near', [(0, 1), (1, 0)])]
  transfers between devices with their start and end apart: 1 -> 2, of which waited for: 1 -> 2; matrix products, arithmetic and copies ran while one was open for 0% -> 0% of each run, Pallas kernels for 0% -> 0%
where the time goes in v3:
time: 95.8 us; the launch traced here: 94.4 us
  blocking collectives  71.9 us (75%)
  Pallas kernels  9.09 us (9%)
  waiting for transfers between devices  8.47 us (9%)
  starting transfers between devices  3.84 us (4%)
    all_to_all x1, blocking collectives, per_device(): lax.all_to_all(chip_sum, 'chip', split_axis=0, concat_axis=0, axis_index_...  40.8 us
    all_to_all x1, blocking collectives, per_device(): lax.all_to_all(near_sum, 'far', split_axis=0, concat_axis=0, axis_index_g...  31.1 us
    pallas_call x1, Pallas kernels, per_device(): pl.pallas_call(functools.partial(partial_kernel, n_chips, first_chip, flo...  7.29 us
    ppermute x1, waiting for transfers between devices, per_device(): theirs = lax.ppermute(other, 'near', [(0, 1), (1, 0)])  4.58 us
    ppermute x1, waiting for transfers between devices, per_device(): theirs = lax.ppermute(other, 'core', [(0, 1), (1, 0)])  3.89 us
    ppermute x1, starting transfers between devices, per_device(): theirs = lax.ppermute(other, 'core', [(0, 1), (1, 0)])  1.92 us
    ppermute x1, starting transfers between devices, per_device(): theirs = lax.ppermute(other, 'near', [(0, 1), (1, 0)])  1.92 us
  transfers between devices with their start and end apart: 2, of which 2 were waited for; matrix products, arithmetic and copies ran while one was open for 0% of the time, Pallas kernels for 0%

profile of v3, /device:TPU:6, one launch (start us, length us, event | category | flops | bytes accessed | tf_op | source)
XLA Modules:
  0.0 94.4 jit_solution(3181501942440218896)
XLA Ops:
  0.6 7.3 %partial_gradients.1 = (f32[16,472,128]{2,1,0:T(8,128)S(1)}, bf16[16,472,128]{2,1,0:T(8,128)(2,1)S(1)}) custom-call(s32[1]{0:T(128)} %bitcast.place_ref, f32[3]{0:T(128)} %params_hbm.1, bf16[512,1152]{1,0:T(8,128)(2,1)} %img_hbm.1, bf16[512,1152]{1,0:T(8,128)(2,1)} %txt_hbm.1, bf16[512,1152]{1,0:T(8,128)(2,1)} %feats_hbm.1, s32[1,512]{1,0:T(1,128)} %bitcast.3, ...), custom_call_target="tpu_custom_call" | custom-call | tf_op jit(solution)/shard_map/partial_gradients/pallas_call | solution.py:226
  7.9 1.9 %collective-permute-start = (bf16[16,472,128]{2,1,0:T(8,128)(2,1)S(1)}, bf16[16,472,128]{2,1,0:T(8,128)(2,1)S(1)}, u32[]{:S(2)}, u32[]{:S(2)}) collective-permute-start(bf16[16,472,128]{2,1,0:T(8,128)(2,1)S(1)} %get-tuple-element.7), channel_id=1, source_target_pairs={{0,1},{1,0},{2,3},{3,2},{4,5},{5,4},{6,7},{7,6},{8,9},{9,8},{10,11... | collective-permute-start | bytes 5799944 | tf_op jit(solution)/shard_map/ppermute | solution.py:257
  9.9 3.9 %collective-permute-done = bf16[16,472,128]{2,1,0:T(8,128)(2,1)S(1)} collective-permute-done((bf16[16,472,128]{2,1,0:T(8,128)(2,1)S(1)}, bf16[16,472,128]{2,1,0:T(8,128)(2,1)S(1)}, u32[]{:S(2)}, u32[]{:S(2)}) %collective-permute-start) | collective-permute-done | bytes 1933344 | tf_op jit(solution)/shard_map/ppermute | solution.py:257
  13.8 0.5 add_convert_fusion
  14.2 0.0 copy-start
  14.2 40.8 %all_to_all.10.parts_ref = bf16[16,472,128]{2,1,0:T(8,128)(2,1)S(1)} all-to-all(bf16[16,472,128]{2,1,0:T(8,128)(2,1)S(1)} %add_convert_fusion), channel_id=1, replica_groups={{20,22,24,26,28,30,0,2,4,6,8,10,12,14,16,18},{21,23,25,27,29,31,1,3,5,7..., dimensions={0} | all-to-all | bytes 3866624 | tf_op jit(solution)/shard_map/all_to_all | solution.py:259
  55.0 0.0 copy-done
  55.0 1.0 %project_blocks.1 = (f32[16,24,128]{2,1,0:T(8,128)S(1)}, bf16[16,24,128]{2,1,0:T(8,128)(2,1)S(1)}) custom-call(s32[1]{0:T(128)} %bitcast.place_ref, bf16[16,472,128]{2,1,0:T(8,128)(2,1)S(1)} %all_to_all.10.parts_ref, bf16[512,1152]{1,0:T(8,128)(2,1)S(1)} %copy-done), custom_call_target="tpu_custom_call" | custom-call | tf_op jit(solution)/shard_map/project_blocks/pallas_call | solution.py:269
  56.0 1.9 %collective-permute-start.1 = (bf16[16,24,128]{2,1,0:T(8,128)(2,1)S(1)}, bf16[16,24,128]{2,1,0:T(8,128)(2,1)S(1)}, u32[]{:S(2)}, u32[]{:S(2)}) collective-permute-start(bf16[16,24,128]{2,1,0:T(8,128)(2,1)S(1)} %get-tuple-element.9), channel_id=1, source_target_pairs={{0,32},{32,0},{1,33},{33,1},{2,34},{34,2},{3,35},{35,3},{4,36},{36... | collective-permute-start | bytes 294920 | tf_op jit(solution)/shard_map/ppermute | solution.py:282
  57.9 4.6 %collective-permute-done.1 = bf16[16,24,128]{2,1,0:T(8,128)(2,1)S(1)} collective-permute-done((bf16[16,24,128]{2,1,0:T(8,128)(2,1)S(1)}, bf16[16,24,128]{2,1,0:T(8,128)(2,1)S(1)}, u32[]{:S(2)}, u32[]{:S(2)}) %collective-permute-start.1) | collective-permute-done | bytes 98336 | tf_op jit(solution)/shard_map/ppermute | solution.py:282
  62.5 31.1 %all_to_all.11.parts_ref = bf16[16,24,128]{2,1,0:T(8,128)(2,1)S(1)} all-to-all(bf16[16,24,128]{2,1,0:T(8,128)(2,1)S(1)} %add_convert_fusion.1), channel_id=1, replica_groups={{512,576,640,704,768,832,896,960,0,64,128,192,256,320,384,448},{513,577..., dimensions={0} | all-to-all | bytes 196608 | tf_op jit(solution)/shard_map/all_to_all | solution.py:284
  93.6 0.8 sum_blocks.1
  (1 shorter events, 0.0 us)
Async XLA Ops:
  7.9 5.8 %collective-permute-start = (bf16[16,472,128]{2,1,0:T(8,128)(2,1)S(1)}, bf16[16,472,128]{2,1,0:T(8,128)(2,1)S(1)}, u32[]{:S(2)}, u32[]{:S(2)}) collective-permute-start(bf16[16,472,128]{2,1,0:T(8,128)(2,1)S(1)} %get-tuple-element.7), channel_id=1, source_target_pairs={{0,1},{1,0},{2,3},{3,2},{4,5},{5,4},{6,7},{7,6},{8,9},{9,8},{10,11... | collective-permute-start | bytes 5799944 | tf_op jit(solution)/shard_map/ppermute | solution.py:257
  14.2 40.8 %copy-start = (bf16[512,1152]{1,0:T(8,128)(2,1)S(1)}, bf16[512,1152]{1,0:T(8,128)(2,1)}, u32[]{:S(2)}) copy-start(bf16[512,1152]{1,0:T(8,128)(2,1)} %feats_ref.1) | copy-start | bytes 3538948
  56.0 6.5 %collective-permute-start.1 = (bf16[16,24,128]{2,1,0:T(8,128)(2,1)S(1)}, bf16[16,24,128]{2,1,0:T(8,128)(2,1)S(1)}, u32[]{:S(2)}, u32[]{:S(2)}) collective-permute-start(bf16[16,24,128]{2,1,0:T(8,128)(2,1)S(1)} %get-tuple-element.9), channel_id=1, source_target_pairs={{0,32},{32,0},{1,33},{33,1},{2,34},{34,2},{3,35},{35,3},{4,36},{36... | collective-permute-start | bytes 294920 | tf_op jit(solution)/shard_map/ppermute | solution.py:282

commit v4 on v3

--- a/solution.py
+++ b/solution.py
@@ -128,7 +128,6 @@
     parts_ref,
     feats_ref,
     mine_ref,
-    other_ref,
     rows_ref,
     total_ref,
     blocks_ref,
@@ -158,7 +157,7 @@
         [projected[0:block], text, jnp.zeros((128 - 2 * block, width), F32)], axis=0
     )
     rows_ref[...] = both.T
-    first = mine_ref.shape[1]
+    first = mine_ref.shape[2]
     n_near, n_far = blocks_ref.shape[0:2]
     rest = block - first
     lane = lax.broadcasted_iota(jnp.int32, (first, 128), 1)
@@ -170,9 +169,7 @@
         )
         place = (target // n_near - first_far) % n_far
         blocks_ref[target % n_near, place] = jnp.where(lane < 2 * block, top, tail)
-    near = place_ref[0] // 2
-    mine_ref[...] = blocks_ref[near]
-    other_ref[...] = blocks_ref[1 - near].astype(other_ref.dtype)
+    mine_ref[...] = blocks_ref[...].astype(mine_ref.dtype)
 
 
 def total_kernel(block, place_ref, parts_ref, img_ref, txt_ref):
@@ -266,11 +263,11 @@
     )
     first_far = n_far // 2
     shape = (n_far, 2 * block // 3, 128)
-    mine, other = pl.pallas_call(
+    blocks = pl.pallas_call(
         functools.partial(project_kernel, first_far, block),
-        out_shape=(jax.ShapeDtypeStruct(shape, F32), jax.ShapeDtypeStruct(shape, BF16)),
+        out_shape=jax.ShapeDtypeStruct((n_near,) + shape, BF16),
         in_specs=[scalar_spec()] + [whole_spec()] * 2,
-        out_specs=[whole_spec()] * 2,
+        out_specs=whole_spec(),
         scratch_shapes=[
             pltpu.VMEM((width, 128), F32),
             pltpu.VMEM((block // 8 * 8 + 8, lanes), F32),
@@ -279,8 +276,8 @@
         compiler_params=compiler_params(16),
         name="project_blocks",
     )(place, parts, img_feats)
-    theirs = lax.ppermute(other, "near", [(0, 1), (1, 0)])
-    near_sum = (mine + theirs.astype(F32)).astype(BF16)
+    near_parts = lax.all_to_all(blocks, "near", split_axis=0, concat_axis=0, tiled=True)
+    near_sum = jnp.sum(near_parts.astype(F32), axis=0).astype(BF16)
     loop_parts = lax.all_to_all(
         near_sum, "far", split_axis=0, concat_axis=0, axis_index_groups=[turned(n_far, first_far)], tiled=True
     )
@@ -296,7 +293,7 @@
 
 def solution(mesh):
     shape = mesh.shape
-    near = 2
+    near = 4
     sizes = (shape["dp"] // near, near, shape["dom"] * shape["mp"] // 2, 2)
     mesh = Mesh(np.asarray(mesh.devices).reshape(sizes), ("far", "near", "chip", "core"))
     loop = ("far", "near")

time: 95.8 us -> 94.9 us (level)
  blocking collectives: 71.9 us -> 77.6 us
  waiting for transfers between devices: 8.47 us -> 3.89 us
  starting transfers between devices: 3.84 us -> 1.92 us
    all_to_all x0 -> x1, blocking collectives: none -> 9.17 us  [per_device(): lax.all_to_all(blocks, 'near', split_axis=0, concat_axis=0, tiled=True)]
    ppermute x1 -> x0, waiting for transfers between devices: 4.58 us -> none  [per_device(): theirs = lax.ppermute(other, 'near', [(0, 1), (1, 0)])]
    all_to_all x1, blocking collectives: 31.1 us -> 27.6 us  [per_device(): lax.all_to_all(near_sum, 'far', split_axis=0, concat_axis=0, axis_index_g...]
    ppermute x1 -> x0, starting transfers between devices: 1.92 us -> none  [per_device(): theirs = lax.ppermute(other, 'near', [(0, 1), (1, 0)])]
  transfers between devices with their start and end apart: 2 -> 1, of which waited for: 2 -> 1; matrix products, arithmetic and copies ran while one was open for 0% -> 0% of each run, Pallas kernels for 0% -> 0%
where the time goes in v4:
time: 94.9 us; the launch traced here: 93.6 us
  blocking collectives  77.6 us (82%)
  Pallas kernels  9.02 us (10%)
  waiting for transfers between devices  3.89 us (4%)
  starting transfers between devices  1.92 us (2%)
    all_to_all x1, blocking collectives, per_device(): lax.all_to_all(chip_sum, 'chip', split_axis=0, concat_axis=0, axis_index_...  40.8 us
    all_to_all x1, blocking collectives, per_device(): lax.all_to_all(near_sum, 'far', split_axis=0, concat_axis=0, axis_index_g...  27.6 us
    all_to_all x1, blocking collectives, per_device(): lax.all_to_all(blocks, 'near', split_axis=0, concat_axis=0, tiled=True)  9.17 us
    pallas_call x1, Pallas kernels, per_device(): pl.pallas_call(functools.partial(partial_kernel, n_chips, first_chip, flo...  7.29 us
    ppermute x1, waiting for transfers between devices, per_device(): theirs = lax.ppermute(other, 'core', [(0, 1), (1, 0)])  3.89 us
    ppermute x1, starting transfers between devices, per_device(): theirs = lax.ppermute(other, 'core', [(0, 1), (1, 0)])  1.92 us
  transfers between devices with their start and end apart: 1, of which 1 were waited for; matrix products, arithmetic and copies ran while one was open for 0% of the time, Pallas kernels for 0%

profile of v4, /device:TPU:6, one launch (start us, length us, event | category | flops | bytes accessed | tf_op | source)
XLA Modules:
  0.0 93.6 jit_solution(8611223866504518645)
XLA Ops:
  0.6 7.3 %partial_gradients.1 = (f32[16,472,128]{2,1,0:T(8,128)S(1)}, bf16[16,472,128]{2,1,0:T(8,128)(2,1)S(1)}) custom-call(s32[1]{0:T(128)} %bitcast.place_ref, f32[3]{0:T(128)} %params_hbm.1, bf16[512,1152]{1,0:T(8,128)(2,1)} %img_hbm.1, bf16[512,1152]{1,0:T(8,128)(2,1)} %txt_hbm.1, bf16[512,1152]{1,0:T(8,128)(2,1)} %feats_hbm.1, s32[1,512]{1,0:T(1,128)} %bitcast.3, ...), custom_call_target="tpu_custom_call" | custom-call | tf_op jit(solution)/shard_map/partial_gradients/pallas_call | solution.py:223
  7.9 1.9 %collective-permute-start = (bf16[16,472,128]{2,1,0:T(8,128)(2,1)S(1)}, bf16[16,472,128]{2,1,0:T(8,128)(2,1)S(1)}, u32[]{:S(2)}, u32[]{:S(2)}) collective-permute-start(bf16[16,472,128]{2,1,0:T(8,128)(2,1)S(1)} %get-tuple-element.5), channel_id=1, source_target_pairs={{0,1},{1,0},{2,3},{3,2},{4,5},{5,4},{6,7},{7,6},{8,9},{9,8},{10,11... | collective-permute-start | bytes 5799944 | tf_op jit(solution)/shard_map/ppermute | solution.py:254
  9.9 3.9 %collective-permute-done = bf16[16,472,128]{2,1,0:T(8,128)(2,1)S(1)} collective-permute-done((bf16[16,472,128]{2,1,0:T(8,128)(2,1)S(1)}, bf16[16,472,128]{2,1,0:T(8,128)(2,1)S(1)}, u32[]{:S(2)}, u32[]{:S(2)}) %collective-permute-start) | collective-permute-done | bytes 1933344 | tf_op jit(solution)/shard_map/ppermute | solution.py:254
  13.8 0.5 add_convert_fusion
  14.2 0.0 copy-start
  14.2 40.8 %all_to_all.15.parts_ref = bf16[16,472,128]{2,1,0:T(8,128)(2,1)S(1)} all-to-all(bf16[16,472,128]{2,1,0:T(8,128)(2,1)S(1)} %add_convert_fusion), channel_id=1, replica_groups={{20,22,24,26,28,30,0,2,4,6,8,10,12,14,16,18},{21,23,25,27,29,31,1,3,5,7..., dimensions={0} | all-to-all | bytes 3866624 | tf_op jit(solution)/shard_map/all_to_all | solution.py:256
  55.0 0.0 copy-done
  55.0 0.9 project_blocks.1
  55.9 9.2 %all_to_all.16 = bf16[4,8,24,128]{3,2,1,0:T(8,128)(2,1)S(1)} all-to-all(bf16[4,8,24,128]{3,2,1,0:T(8,128)(2,1)S(1)} %project_blocks.1), channel_id=1, replica_groups=mesh['far'=8,'near'=4,'chip'=16,'core'=2] {'near'}, dimensions={0} | all-to-all | bytes 393216 | tf_op jit(solution)/shard_map/all_to_all | solution.py:279
  65.1 27.6 %all_to_all.17.parts_ref = bf16[8,24,128]{2,1,0:T(8,128)(2,1)S(1)} all-to-all(bf16[8,24,128]{2,1,0:T(8,128)(2,1)S(1)} %reduce_sum.12), channel_id=1, replica_groups={{512,640,768,896,0,128,256,384},{513,641,769,897,1,129,257,385},{514,64..., dimensions={0} | all-to-all | bytes 98304 | tf_op jit(solution)/shard_map/all_to_all | solution.py:281
  92.8 0.8 sum_blocks.1
  (1 shorter events, 0.0 us)
Async XLA Ops:
  7.9 5.8 %collective-permute-start = (bf16[16,472,128]{2,1,0:T(8,128)(2,1)S(1)}, bf16[16,472,128]{2,1,0:T(8,128)(2,1)S(1)}, u32[]{:S(2)}, u32[]{:S(2)}) collective-permute-start(bf16[16,472,128]{2,1,0:T(8,128)(2,1)S(1)} %get-tuple-element.5), channel_id=1, source_target_pairs={{0,1},{1,0},{2,3},{3,2},{4,5},{5,4},{6,7},{7,6},{8,9},{9,8},{10,11... | collective-permute-start | bytes 5799944 | tf_op jit(solution)/shard_map/ppermute | solution.py:254
  14.2 40.8 %copy-start = (bf16[512,1152]{1,0:T(8,128)(2,1)S(1)}, bf16[512,1152]{1,0:T(8,128)(2,1)}, u32[]{:S(2)}) copy-start(bf16[512,1152]{1,0:T(8,128)(2,1)} %feats_ref.1) | copy-start | bytes 3538948
